TPU v7x, 512 devices: a whole 4x8x8 slice. The times are simulated.
512 devices in a mesh: depth: 16 (over y, core), tile: 32 (over z, x).
Axes of the slice: x: 4, y: 8, z: 8, core: 2. Of those that a mesh axis runs over, the one named last changes fastest.
Arguments:
- colour: bfloat16 [16, 3, 4096, 4096], P('depth', None, 'tile'), may hold values from -6 to 6
- alpha: bfloat16 [16, 4096, 4096], P('depth', 'tile'), may hold values from 0.049804688 to 0.5
- depth_order: int32 [16], replicated, may hold values from 0 to 15, as said below
- row_taps: int32 [4, 4096], P(None, 'tile'), may hold values from 0 to 383, as said below
- row_weights: bfloat16 [4, 4096], P(None, 'tile'), may hold values from -0.25 to 0.75
- col_taps: int32 [4, 4, 4096], P(None, None, 'depth'), may hold values from 0 to 4095, as said below
- col_weights: bfloat16 [4, 4, 4096], P(None, None, 'depth'), may hold values from -0.25 to 0.75
- colour_matrix: float32 [4, 3, 3], replicated
- offsets: float32 [4, 3], replicated, may hold values from -0.5 to 0.5
Outputs:
- projected: float32 [3, 4096, 4096], P(None, 'tile', 'depth')
Inputs may be any that keep to these rules, and one draw needn't show every extreme that they name: depth_order[k] = f XOR b(k), where b(k) reverses the order of the bits of k over the 16 values and f is one number of 0 to 15: the groups are the leaves of a binary space partition, visited front to back. `row_taps`: the four taps of an output row are consecutive rows, rising by one; within a band the first tap minus the output row's place in its band is the same for all rows. `col_taps`: the four taps of an output column x are consecutive columns, rising by one, all within 128 columns of x.
All inputs are finite; a program needn't handle non-finite values.
Results may differ from a plain program's by a relative error of at most 0.0038.
Values may be sent and summed in bfloat16 or wider, within the bound.
A program may use at most 64 MiB of HBM per device.

v0:
```python
import jax
import jax.numpy as jnp
from jax import lax
from jax.sharding import PartitionSpec as P

HC = 128
BLEND = 64


def padded(block, sides, width):
    for axis, dim in sides:
        count = lax.axis_size(axis)
        forward = [(i, i + 1) for i in range(count - 1)]
        backward = [(target, source) for source, target in forward]
        low = lax.ppermute(
            lax.slice_in_dim(block, block.shape[dim] - width, None, axis=dim), axis, forward
        )
        high = lax.ppermute(lax.slice_in_dim(block, 0, width, axis=dim), axis, backward)
        block = jnp.concatenate([low, block, high], axis=dim)
    return block


def shards(
    colour, alpha, depth_order, row_taps, row_weights, col_taps, col_weights, colour_matrix, offsets
):
    groups = lax.axis_size("depth")
    height = colour.shape[2]
    width_cols = colour.shape[3]
    slab_cols = width_cols // groups
    layer_colours, layer_alphas = (
        lax.all_to_all(colour, "depth", split_axis=3, concat_axis=0, tiled=True),
        lax.all_to_all(alpha[:, None], "depth", split_axis=3, concat_axis=0, tiled=True),
    )
    accumulated = jnp.zeros((3, height, slab_cols), jnp.float32)
    remaining = jnp.ones((1, height, slab_cols), jnp.float32)
    for position in range(groups):
        group_id = depth_order[position]
        layer_colour = lax.dynamic_index_in_dim(layer_colours, group_id, 0, keepdims=False).astype(
            jnp.float32
        )
        layer_alpha = lax.dynamic_index_in_dim(layer_alphas, group_id, 0, keepdims=False).astype(
            jnp.float32
        )
        accumulated = accumulated + remaining * layer_colour
        remaining = remaining * (1.0 - layer_alpha)
    composite = accumulated.astype(jnp.bfloat16)
    extended = padded(composite, (("tile", 1),), height)
    matches_rows = row_taps[:, :, None] == jnp.arange(3 * height)[None, None, :]
    row_matrix = jnp.sum(
        jnp.where(matches_rows, row_weights.astype(jnp.float32)[:, :, None], 0.0), axis=0
    ).astype(jnp.bfloat16)
    widened = padded(extended, (("depth", 2),), HC)
    vertical = jnp.einsum(
        "ri,cix->crx", row_matrix, widened, preferred_element_type=jnp.float32
    ).astype(jnp.bfloat16)
    tile_index = lax.axis_index("tile")
    bands = lax.axis_size("tile") // colour_matrix.shape[0]
    proj_index = tile_index // bands
    tap_cols = lax.dynamic_index_in_dim(col_taps, proj_index, 0, keepdims=False)
    weight_cols = lax.dynamic_index_in_dim(col_weights, proj_index, 0, keepdims=False)
    first_col = lax.axis_index("depth") * slab_cols - HC
    local_cols = tap_cols - first_col
    matches_cols = local_cols[:, None, :] == jnp.arange(slab_cols + 2 * HC)[None, :, None]
    col_matrix = jnp.sum(
        jnp.where(matches_cols, weight_cols.astype(jnp.float32)[:, None, :], 0.0), axis=0
    ).astype(jnp.bfloat16)
    warped = jnp.dot(
        vertical.reshape(3 * height, slab_cols + 2 * HC),
        col_matrix,
        preferred_element_type=jnp.float32,
    ).reshape(3, height, slab_cols)
    row_index = jnp.arange(height).astype(jnp.float32)
    proj_height = bands * height
    within = (tile_index % bands * height).astype(jnp.float32) + row_index
    blend_ramp = jnp.minimum(
        1.0, jnp.minimum((within + 0.5) / BLEND, (proj_height - within - 0.5) / BLEND)
    )
    blended = warped * blend_ramp[None, :, None]
    colour_mix = lax.dynamic_index_in_dim(colour_matrix, proj_index, 0, keepdims=False)
    colour_shift = lax.dynamic_index_in_dim(offsets, proj_index, 0, keepdims=False)
    outputs = []
    for channel in range(3):
        mixed_sum = (
            colour_mix[channel, 0] * blended[0]
            + colour_mix[channel, 1] * blended[1]
            + colour_mix[channel, 2] * blended[2]
        )
        outputs.append(mixed_sum + colour_shift[channel])
    return jnp.stack(outputs)


def solution(mesh):
    return jax.shard_map(
        shards,
        mesh=mesh,
        in_specs=(
            P("depth", None, "tile", None),
            P("depth", "tile", None),
            P(),
            P(None, "tile"),
            P(None, "tile"),
            P(None, None, "depth"),
            P(None, None, "depth"),
            P(),
            P(),
        ),
        out_specs=P(None, "tile", "depth"),
        check_vma=False,
    )
```

profile of v0, /device:TPU:416, one launch (start us, length us, event | category | flops | bytes accessed | tf_op | source)
XLA Modules:
  0.0 199.8 jit_solution(6485575757959255949)
XLA Ops:
  0.0 5.0 %copy.96 = bf16[1,1,128,4096]{2,1,0,3:T(2,128)(2,1)S(1)} copy(bf16[1,1,128,4096]{3,2,1,0:T(8,128)(2,1)} %bitcast.187) | data formatting | bytes 2097152 | tf_op jit(solution)/shard_map/broadcast_in_dim | solution.py:32
  5.6 22.4 %reduce = bf16[4096,128]{1,0:T(8,128)(2,1)S(1)} reduce(bf16[4096,1,1,128]{3,2,1,0:T(2,128)(2,1)S(1)} %bitcast.184, bf16[]{:T(256)} %broadcast.501), dimensions={1,2}, to_apply=%bitcast.165.reduce_sub_computation | reduce | bytes 2097154
  28.0 1.1 reshape.840
  29.1 7.2 %all-to-all-start.1 = ((bf16[16,2,16384]{2,1,0:T(2,128)(2,1)}), bf16[16,2,16384]{2,1,0:T(2,128)(2,1)S(1)}, u32[]{:S(2)}, u32[]{:S(2)}) async-start(bf16[16,2,16384]{2,1,0:T(2,128)(2,1)} %reshape.840), calls=%async_computation.1 | async-start | bytes 2097152 | tf_op jit(solution)/shard_map/all_to_all | solution.py:32
  36.3 7.2 %copy.93 = bf16[1,3,128,4096]{2,1,0,3:T(4,128)(2,1)} copy(bf16[1,3,128,4096]{3,2,1,0:T(8,128)(2,1)} %param.9) | data formatting | bytes 6291456 | tf_op args[0]
  43.4 17.1 %all-to-all-done.1 = bf16[16,2,16384]{2,1,0:T(2,128)(2,1)S(1)} async-done(((bf16[16,2,16384]{2,1,0:T(2,128)(2,1)}), bf16[16,2,16384]{2,1,0:T(2,128)(2,1)S(1)}, u32[]{:S(2)}, u32[]{:S(2)}) %all-to-all-start.1) | async-done | bytes 1048608 | tf_op jit(solution)/shard_map/all_to_all | solution.py:32
  60.5 7.2 %all-to-all-start = ((bf16[1,3,128,4096]{2,1,0,3:T(4,128)(2,1)}), bf16[1,3,128,4096]{2,1,0,3:T(4,128)(2,1)}, u32[]{:S(2)}, u32[]{:S(2)}) async-start(bf16[1,3,128,4096]{2,1,0,3:T(4,128)(2,1)} %copy.93), calls=%async_computation | async-start | bytes 8388608 | tf_op jit(solution)/shard_map/all_to_all | solution.py:31
  67.8 0.7 fusion.52
  100.1 1.0 reshape.841
  101.6 57.9 %all-to-all-done = bf16[1,3,128,4096]{2,1,0,3:T(4,128)(2,1)} async-done(((bf16[1,3,128,4096]{2,1,0,3:T(4,128)(2,1)}), bf16[1,3,128,4096]{2,1,0,3:T(4,128)(2,1)}, u32[]{:S(2)}, u32[]{:S(2)}) %all-to-all-start) | async-done | bytes 3145760 | tf_op jit(solution)/shard_map/all_to_all | solution.py:31
  159.5 2.6 %copy.94 = bf16[1,3,128,4096]{2,3,1,0:T(8,128)(2,1)S(1)} copy(bf16[1,3,128,4096]{2,1,0,3:T(4,128)(2,1)} %all-to-all-done) | data formatting | bytes 6291456 | tf_op jit(solution)/shard_map/all_to_all | solution.py:31
  162.1 0.8 fusion.22
  162.9 4.7 %collective-permute-start.1 = (bf16[3,128,256]{1,2,0:T(8,128)(2,1)S(1)}, bf16[3,128,256]{1,2,0:T(8,128)(2,1)S(1)}, u32[]{:S(2)}, u32[]{:S(2)}) collective-permute-start(bf16[3,128,256]{1,2,0:T(8,128)(2,1)S(1)} %fusion.22), channel_id=1, source_target_pairs={{1,0},{2,1},{3,2},{4,3},{5,4},{6,5},{7,6},{8,7},{9,8},{10,9},{11,1... | collective-permute-start | bytes 589832 | tf_op jit(solution)/shard_map/ppermute | solution.py:18
  167.6 1.9 collective-permute-start
  170.9 1.1 collective-permute-done.1
  172.0 6.2 %collective-permute-done = bf16[3,128,256]{1,2,0:T(8,128)(2,1)S(1)} collective-permute-done((bf16[3,128,256]{1,2,0:T(8,128)(2,1)S(1)}, bf16[3,128,256]{1,2,0:T(8,128)(2,1)S(1)}, u32[]{:S(2)}, u32[]{:S(2)}) %collective-permute-start) | collective-permute-done | bytes 196640 | tf_op jit(solution)/shard_map/ppermute | solution.py:15
  178.4 3.0 %collective-permute-start.3 = (bf16[3,384,128]{1,2,0:T(8,128)(2,1)S(1)}, bf16[3,384,128]{1,2,0:T(8,128)(2,1)S(1)}, u32[]{:S(2)}, u32[]{:S(2)}) collective-permute-start(bf16[3,384,128]{1,2,0:T(8,128)(2,1)S(1)} %get-tuple-element.20), channel_id=1, source_target_pairs={{32,0},{64,32},{96,64},{128,96},{160,128},{192,160},{224,192},{256... | collective-permute-start | bytes 884744 | tf_op jit(solution)/shard_map/ppermute | solution.py:18
  181.5 1.9 collective-permute-start.2
  183.9 1.7 collective-permute-done.3
  185.7 5.0 %collective-permute-done.2 = bf16[3,384,128]{1,2,0:T(8,128)(2,1)S(1)} collective-permute-done((bf16[3,384,128]{1,2,0:T(8,128)(2,1)S(1)}, bf16[3,384,128]{1,2,0:T(8,128)(2,1)S(1)}, u32[]{:S(2)}, u32[]{:S(2)}) %collective-permute-start.2) | collective-permute-done | bytes 294944 | tf_op jit(solution)/shard_map/ppermute | solution.py:15
  190.7 0.8 fusion.2
  191.5 2.4 %add_add_fusion = f32[1,128,256]{2,1,0:T(8,128)S(1)} fusion(f32[3,128,256]{2,1,0:T(8,128)S(1)} %fusion.2, f32[]{:T(128)} %bitcast.65, f32[]{:T(128)} %bitcast.64, f32[]{:T(128)} %bitcast.63, f32[]{:T(128)} %bitcast.62), kind=kLoop, calls=%fused_computation.66 | loop fusion | flops 196608 | bytes 524304 | tf_op jit(solution)/shard_map/add | solution.py:88
  194.0 5.1 %add_add_fusion.2 = (f32[1,128,256]{2,1,0:T(8,128)S(1)}, f32[1,128,256]{2,1,0:T(8,128)S(1)}) fusion(f32[3,128,256]{2,1,0:T(8,128)S(1)} %fusion.2, f32[]{:T(128)} %bitcast.57, f32[]{:T(128)} %bitcast.56, f32[]{:T(128)} %bitcast.55, f32[]{:T(128)} %bitcast, f32[]{:T(128)} %bitcast.61, f32[]{:T(128)} %bitcast.60, f32[]{:T(128)} %bitcast.59, f32[]{:T(128)} %bitcast.58), kind=kLoop, calls=%fused_computation.68 | loop fusion | flops 393216 | bytes 655392 | tf_op jit(solution)/shard_map/add | solution.py:88
  199.1 0.8 pad_maximum_fusion.1
  (25 shorter events, 5.0 us)
Async XLA Ops:
  0.0 88.2 %copy-start = (f32[4,3,3]{2,0,1:T(4,128)S(1)}, f32[4,3,3]{2,0,1:T(4,128)}, u32[]{:S(2)}) copy-start(f32[4,3,3]{2,0,1:T(4,128)} %param.16) | copy-start | bytes 436
  29.1 31.5 %all-to-all-start.1 = ((bf16[16,2,16384]{2,1,0:T(2,128)(2,1)}), bf16[16,2,16384]{2,1,0:T(2,128)(2,1)S(1)}, u32[]{:S(2)}, u32[]{:S(2)}) async-start(bf16[16,2,16384]{2,1,0:T(2,128)(2,1)} %reshape.840), calls=%async_computation.1 | async-start | bytes 2097152 | tf_op jit(solution)/shard_map/all_to_all | solution.py:32
  43.4 24.3 %copy-start.1 = (s32[16]{0:T(128)S(1)}, s32[16]{0:T(128)}, u32[]{:S(2)}) copy-start(s32[16]{0:T(128)} %param.11) | copy-start | bytes 196
  60.5 99.0 %all-to-all-start = ((bf16[1,3,128,4096]{2,1,0,3:T(4,128)(2,1)}), bf16[1,3,128,4096]{2,1,0,3:T(4,128)(2,1)}, u32[]{:S(2)}, u32[]{:S(2)}) async-start(bf16[1,3,128,4096]{2,1,0,3:T(4,128)(2,1)} %copy.93), calls=%async_computation | async-start | bytes 8388608 | tf_op jit(solution)/shard_map/all_to_all | solution.py:31
  162.9 20.5 %copy-start.3 = (bf16[4,128]{1,0:T(4,128)(2,1)S(1)}, bf16[4,128]{1,0:T(4,128)(2,1)}, u32[]{:S(2)}) copy-start(bf16[4,128]{1,0:T(4,128)(2,1)} %param.13) | copy-start | bytes 3076
  162.9 20.5 %copy-start.2 = (s32[4,128]{1,0:T(4,128)S(1)}, s32[4,128]{1,0:T(4,128)}, u32[]{:S(2)}) copy-start(s32[4,128]{1,0:T(4,128)} %param.12) | copy-start | bytes 6148
  162.9 9.1 %collective-permute-start.1 = (bf16[3,128,256]{1,2,0:T(8,128)(2,1)S(1)}, bf16[3,128,256]{1,2,0:T(8,128)(2,1)S(1)}, u32[]{:S(2)}, u32[]{:S(2)}) collective-permute-start(bf16[3,128,256]{1,2,0:T(8,128)(2,1)S(1)} %fusion.22), channel_id=1, source_target_pairs={{1,0},{2,1},{3,2},{4,3},{5,4},{6,5},{7,6},{8,7},{9,8},{10,9},{11,1... | collective-permute-start | bytes 589832 | tf_op jit(solution)/shard_map/ppermute | solution.py:18
  167.6 10.6 %collective-permute-start = (bf16[3,128,256]{1,2,0:T(8,128)(2,1)S(1)}, bf16[3,128,256]{1,2,0:T(8,128)(2,1)S(1)}, u32[]{:S(2)}, u32[]{:S(2)}) collective-permute-start(bf16[3,128,256]{1,2,0:T(8,128)(2,1)S(1)} %fusion.22), channel_id=1, source_target_pairs={{0,1},{1,2},{2,3},{3,4},{4,5},{5,6},{6,7},{7,8},{8,9},{9,10},{10,1... | collective-permute-start | bytes 589832 | tf_op jit(solution)/shard_map/ppermute | solution.py:15
  178.4 7.3 %collective-permute-start.3 = (bf16[3,384,128]{1,2,0:T(8,128)(2,1)S(1)}, bf16[3,384,128]{1,2,0:T(8,128)(2,1)S(1)}, u32[]{:S(2)}, u32[]{:S(2)}) collective-permute-start(bf16[3,384,128]{1,2,0:T(8,128)(2,1)S(1)} %get-tuple-element.20), channel_id=1, source_target_pairs={{32,0},{64,32},{96,64},{128,96},{160,128},{192,160},{224,192},{256... | collective-permute-start | bytes 884744 | tf_op jit(solution)/shard_map/ppermute | solution.py:18
  181.5 9.3 %collective-permute-start.2 = (bf16[3,384,128]{1,2,0:T(8,128)(2,1)S(1)}, bf16[3,384,128]{1,2,0:T(8,128)(2,1)S(1)}, u32[]{:S(2)}, u32[]{:S(2)}) collective-permute-start(bf16[3,384,128]{1,2,0:T(8,128)(2,1)S(1)} %get-tuple-element.19), channel_id=1, source_target_pairs={{0,32},{32,64},{64,96},{96,128},{128,160},{160,192},{192,224},{224... | collective-permute-start | bytes 884744 | tf_op jit(solution)/shard_map/ppermute | solution.py:15
where the time goes:
time: 201 us; the launch traced here: 200 us
  waiting for transfers between devices  89.1 us (44%)
  other arithmetic  33.7 us (17%)
  between operations  29.8 us (15%)
  starting transfers between devices  26 us (13%)
  local copies, waits for them, and re-layouts  20.4 us (10%)
    all_to_all x1, waiting for transfers between devices, shards(): lax.all_to_all(colour, 'depth', split_axis=3, concat_axis=0, tiled=True)  57.9 us
    unnamed x1, other arithmetic  22.4 us
    all_to_all x1, waiting for transfers between devices, shards(): lax.all_to_all(alpha[:, None], 'depth', split_axis=3, concat_axis=0, tile...  17.1 us
    ppermute x2, waiting for transfers between devices, padded(): lax.ppermute(lax.slice_in_dim(block, block.shape[dim] - width, None, axis...  11.3 us
    unnamed x14, local copies, waits for them, and re-layouts  9.98 us
    ppermute x2, starting transfers between devices, padded(): lax.ppermute(lax.slice_in_dim(block, 0, width, axis=dim), axis, backward)  7.7 us
    add x2, other arithmetic, shards(): outputs.append(mixed_sum + colour_shift[channel])  7.53 us
    all_to_all x1, starting transfers between devices, shards(): lax.all_to_all(colour, 'depth', split_axis=3, concat_axis=0, tiled=True)  7.23 us
  transfers between devices with their start and end apart: 6, of which 6 were waited for; matrix products, arithmetic and copies ran while one was open for 7% of the time, Pallas kernels for 0%

commit v1 on v0

v1 whole, which is shorter than its diff:
```python
import functools

import jax
import jax.numpy as jnp
from jax import lax
from jax.experimental import pallas as pl
from jax.experimental.pallas import tpu as pltpu
from jax.sharding import PartitionSpec as P

HC = 128
BLEND = 64
GROUPS = 16
CHIPS = 8
CHUNKS = 4
TILE_ROWS = 16
LANES = 128
STEPS = (4, 5, 3, 6, 2, 7, 1)
MESH = pl.DeviceIdType.MESH
F32 = jnp.float32
BF16 = jnp.bfloat16


def square(x):
    return (x * jnp.abs(x)).astype(BF16)


def root(v):
    v = v.astype(F32)
    return v * lax.rsqrt(jnp.maximum(jnp.abs(v), 1e-37))


def kernel(
    bands_per_projector,
    tiles,
    colour, alpha, order, row_taps, row_weights, col_taps, col_weights, matrix, offsets,
    out,
    opac, cols, remain_out, remain_in, part_out, part_in, window, low, vert,
    a_send, a_recv, a_own, c_own, c_send, c_recv, r_send, r_recv, p_send, p_recv,
    h_send, h_recv, v_send, v_recv,
):
    height, slab = out.shape[1], out.shape[2]
    chunk = height // CHUNKS
    blocks = (chunk // TILE_ROWS) * (slab // LANES)
    d = lax.axis_index("depth")
    t = lax.axis_index("tile")
    y, c = d // 2, d % 2
    sigma = 1 - 2 * c
    sibling = 2 * y + 1 - c
    below, above = (t + 1) % tiles, (t + tiles - 1) % tiles

    def chip(offset):
        return (y + offset + 2 * CHIPS) % CHIPS

    def columns(device):
        return pl.ds(pl.multiple_of(device * slab, slab), slab)

    def rows_of(k):
        return pl.ds(pl.multiple_of(k * chunk, chunk), chunk)

    barrier = pltpu.get_barrier_semaphore()

    def greet(i, _):
        pl.semaphore_signal(barrier, 1, device_id=((d + i) % GROUPS, t), device_id_type=MESH)
        return 0

    lax.fori_loop(1, GROUPS, greet, 0)
    pl.semaphore_signal(barrier, 1, device_id=(d, below), device_id_type=MESH)
    pl.semaphore_signal(barrier, 1, device_id=(d, above), device_id_type=MESH)

    def own_alpha(k):
        return pltpu.make_async_copy(
            alpha.at[0, rows_of(k), columns(d)], opac.at[k, d], a_own.at[k]
        )

    def own_colour(s):
        return pltpu.make_async_copy(
            colour.at[0, :, :, columns(2 * s + c)], cols.at[c, s], c_own.at[s]
        )

    def loop(n, body):
        def step(i, _):
            body(i)
            return 0

        lax.fori_loop(0, n, step, 0)

    loop(CHUNKS, lambda k: own_alpha(k).start())
    loop(CHIPS, lambda s: own_colour(s).start())
    pl.semaphore_wait(barrier, GROUPS + 1)

    def send_alpha(k, i):
        to = (d + i) % GROUPS
        return pltpu.make_async_remote_copy(
            src_ref=alpha.at[0, rows_of(k), columns(to)],
            dst_ref=opac.at[k, d],
            send_sem=a_send.at[k, i],
            recv_sem=a_recv.at[k, i],
            device_id=(to, t),
            device_id_type=MESH,
        )

    def recv_alpha(k, i):
        source = (d + GROUPS - i) % GROUPS
        return pltpu.make_async_remote_copy(
            src_ref=alpha.at[0, rows_of(k), columns(source)],
            dst_ref=opac.at[k, source],
            send_sem=a_send.at[k, i],
            recv_sem=a_recv.at[k, i],
            device_id=(source, t),
            device_id_type=MESH,
        )

    def send_colour(s):
        return pltpu.make_async_remote_copy(
            src_ref=colour.at[0, :, :, columns(2 * s + 1 - c)],
            dst_ref=cols.at[c, s],
            send_sem=c_send.at[s],
            recv_sem=c_recv.at[s],
            device_id=(sibling, t),
            device_id_type=MESH,
        )

    def recv_colour(s):
        return pltpu.make_async_remote_copy(
            src_ref=colour.at[0, :, :, columns(2 * s + 1 - c)],
            dst_ref=cols.at[1 - c, s],
            send_sem=c_send.at[s],
            recv_sem=c_recv.at[s],
            device_id=(sibling, t),
            device_id_type=MESH,
        )

    def send_remain(k, j):
        to = chip(sigma * j)
        return pltpu.make_async_remote_copy(
            src_ref=remain_out.at[k, to],
            dst_ref=remain_in.at[k, j],
            send_sem=r_send.at[k, j],
            recv_sem=r_recv.at[k, j],
            device_id=(2 * to + c, t),
            device_id_type=MESH,
        )

    def send_part(k, j):
        to = chip(-sigma) if j <= 4 else chip(sigma)
        return pltpu.make_async_remote_copy(
            src_ref=part_out.at[k, j],
            dst_ref=part_in.at[k, j - 1 if j <= 4 else j + 1],
            send_sem=p_send.at[k, j],
            recv_sem=p_recv.at[k, j - 1 if j <= 4 else j + 1],
            device_id=(2 * to + c, t),
            device_id_type=MESH,
        )

    def recv_part(k, slot):
        return pltpu.make_async_remote_copy(
            src_ref=part_out.at[k, 1],
            dst_ref=part_in.at[k, slot],
            send_sem=p_send.at[k, 1],
            recv_sem=p_recv.at[k, slot],
            device_id=(sibling, t),
            device_id_type=MESH,
        )

    def send_halo(k, side):
        middle = window.at[:, pl.ds(pl.multiple_of(height + k * chunk, chunk), chunk), :]
        at = 2 * height if side == 0 else 0
        return pltpu.make_async_remote_copy(
            src_ref=middle,
            dst_ref=window.at[:, pl.ds(pl.multiple_of(at + k * chunk, chunk), chunk), :],
            send_sem=h_send.at[k, side],
            recv_sem=h_recv.at[k, side],
            device_id=(d, above if side == 0 else below),
            device_id_type=MESH,
        )

    def send_beside(side):
        to = (d + GROUPS - 1) % GROUPS if side == 0 else (d + 1) % GROUPS
        source = HC if side == 0 else slab
        target = HC + slab if side == 0 else 0
        return pltpu.make_async_remote_copy(
            src_ref=vert.at[:, :, pl.ds(source, HC)],
            dst_ref=vert.at[:, :, pl.ds(target, HC)],
            send_sem=v_send.at[side],
            recv_sem=v_recv.at[side],
            device_id=(to, t),
            device_id_type=MESH,
        )

    def every(first, last, body):
        def outer(k, _):
            def inner(i, _):
                body(k, i)
                return 0

            return lax.fori_loop(first, last, inner, 0)

        lax.fori_loop(0, CHUNKS, outer, 0)

    every(1, GROUPS, lambda k, i: send_alpha(k, i).start())
    loop(CHIPS, lambda s: send_colour(s).start())

    flips = [(order[0] // (1 << bit)) % 2 for bit in range(4)]

    def in_front(bit, value, hidden):
        return jnp.where(flips[bit] == value, 1.0, hidden)

    def block_at(b):
        lanes = slab // LANES
        return (
            pl.multiple_of((b // lanes) * TILE_ROWS, TILE_ROWS),
            pl.multiple_of((b % lanes) * LANES, LANES),
        )

    def remains(k):
        own_alpha(k).wait()
        loop(GROUPS - 1, lambda i: recv_alpha(k, i + 1).wait_recv())

        def block(b):
            row, lane = block_at(b)
            place = (pl.ds(row, TILE_ROWS), pl.ds(lane, LANES))
            clear = [1.0 - opac[(k, g) + place].astype(F32) for g in range(GROUPS)]
            eight = [clear[g] * clear[g + 8] for g in range(8)]
            four = [eight[g] * eight[g + 4] for g in range(4)]
            two = [four[g] * four[g + 2] for g in range(2)]
            left = [in_front(0, g, two[1 - g]) for g in range(2)]
            left = [left[g % 2] * in_front(1, g // 2, four[g ^ 2]) for g in range(4)]
            left = [left[g % 4] * in_front(2, g // 4, eight[g ^ 4]) for g in range(8)]
            for g in range(GROUPS):
                value = left[g % 8] * in_front(3, g // 8, clear[g ^ 8])
                remain_out[(k, g // 2, g % 2) + place] = (value * value).astype(BF16)

        loop(blocks, block)
        loop(CHIPS - 1, lambda i: send_remain(k, i + 1).start())

    loop(CHUNKS, remains)

    loop(CHIPS, lambda s: own_colour(s).wait())
    loop(CHIPS, lambda s: recv_colour(s).wait_recv())

    def add_step(j):
        s = chip(-sigma * j)

        def of_chunk(k):
            send_remain(k, j).wait_recv()
            if j not in (4, 5):
                recv_part(k, j).wait_recv()

            def block(b):
                row, lane = block_at(b)
                place = (pl.ds(row, TILE_ROWS), pl.ds(lane, LANES))
                whole = (pl.ds(pl.multiple_of(k * chunk + row, TILE_ROWS), TILE_ROWS), pl.ds(lane, LANES))
                first = root(remain_in[(k, j, 0) + place])
                second = root(remain_in[(k, j, 1) + place])
                for channel in range(3):
                    total = first * cols[(0, s, channel) + whole].astype(F32)
                    total += second * cols[(1, s, channel) + whole].astype(F32)
                    if j not in (4, 5):
                        total += root(part_in[(k, j, channel) + place])
                    part_out[(k, j, channel) + place] = square(total)

            loop(blocks, block)
            send_part(k, j).start()

        loop(CHUNKS, of_chunk)

    for j in STEPS:
        add_step(j)

    def finish(k):
        recv_part(k, 0).wait_recv()
        recv_part(k, 8).wait_recv()

        def block(b):
            row, lane = block_at(b)
            place = (pl.ds(row, TILE_ROWS), pl.ds(lane, LANES))
            whole_row = pl.multiple_of(k * chunk + row, TILE_ROWS)
            whole = (pl.ds(whole_row, TILE_ROWS), pl.ds(lane, LANES))
            middle = (pl.ds(pl.multiple_of(height + whole_row, TILE_ROWS), TILE_ROWS), pl.ds(lane, LANES))
            first = root(remain_out[(k, y, 0) + place])
            second = root(remain_out[(k, y, 1) + place])
            for channel in range(3):
                total = first * cols[(0, y, channel) + whole].astype(F32)
                total += second * cols[(1, y, channel) + whole].astype(F32)
                total += root(part_in[(k, 0, channel) + place])
                total += root(part_in[(k, 8, channel) + place])
                high = total.astype(BF16)
                window[(channel,) + middle] = high
                low[(channel,) + whole] = (total - high.astype(F32)).astype(BF16)

        loop(blocks, block)
        send_halo(k, 0).start()
        send_halo(k, 1).start()

    loop(CHUNKS, finish)

    place = lax.broadcasted_iota(jnp.int32, (3 * height, height), 0)
    picks = jnp.zeros((3 * height, height), F32)
    for tap in range(4):
        taps = row_taps[tap, :][None, :]
        picks += jnp.where(taps == place, row_weights[tap, :].astype(F32)[None, :], 0.0)
    outside = ((place < height) & (t == 0)) | ((place >= 2 * height) & (t == tiles - 1))
    picks = jnp.transpose(jnp.where(outside, 0.0, picks)).astype(BF16)

    width = slab + 2 * HC
    p = t // bands_per_projector
    place = lax.broadcasted_iota(jnp.int32, (width, slab), 0) + (d * slab - HC)
    col_picks = jnp.zeros((width, slab), F32)
    for tap in range(4):
        taps = col_taps[p, tap, :][None, :]
        col_picks += jnp.where(taps == place, col_weights[p, tap, :].astype(F32)[None, :], 0.0)
    col_picks = col_picks.astype(BF16)

    def wait_halo(k):
        send_halo(k, 0).wait_recv()
        send_halo(k, 1).wait_recv()

    loop(CHUNKS, wait_halo)

    for channel in range(3):
        value = jnp.dot(picks, window[channel], preferred_element_type=F32)
        value += jnp.dot(picks[:, height : 2 * height], low[channel], preferred_element_type=F32)
        vert[channel, :, HC : HC + slab] = value.astype(BF16)
    send_beside(0).start()
    send_beside(1).start()

    within = (t % bands_per_projector) * height + lax.broadcasted_iota(jnp.int32, (height, slab), 0)
    within = within.astype(F32)
    proj_height = bands_per_projector * height
    ramp = jnp.minimum(
        1.0, jnp.minimum((within + 0.5) / BLEND, (proj_height - within - 0.5) / BLEND)
    )

    send_beside(0).wait_recv()
    send_beside(1).wait_recv()
    blended = [
        jnp.dot(vert[channel], col_picks, preferred_element_type=F32) * ramp for channel in range(3)
    ]
    for channel in range(3):
        mixed = matrix[p, channel, 0] * blended[0]
        mixed += matrix[p, channel, 1] * blended[1]
        mixed += matrix[p, channel, 2] * blended[2]
        out[channel] = mixed + offsets[p, channel]

    every(1, GROUPS, lambda k, i: send_alpha(k, i).wait_send())
    loop(CHIPS, lambda s: send_colour(s).wait_send())
    every(1, CHIPS, lambda k, j: send_remain(k, j).wait_send())
    for j in STEPS:
        loop(CHUNKS, lambda k: send_part(k, j).wait_send())
    loop(CHUNKS, lambda k: send_halo(k, 0).wait_send())
    loop(CHUNKS, lambda k: send_halo(k, 1).wait_send())
    send_beside(0).wait_send()
    send_beside(1).wait_send()


def shards(
    colour, alpha, depth_order, row_taps, row_weights, col_taps, col_weights, colour_matrix, offsets
):
    tiles = lax.axis_size("tile")
    height = colour.shape[2]
    slab = colour.shape[3] // GROUPS
    chunk = height // CHUNKS
    hbm = pl.BlockSpec(memory_space=pltpu.HBM)
    vmem = pl.BlockSpec(memory_space=pltpu.VMEM)
    smem = pl.BlockSpec(memory_space=pltpu.SMEM)
    dma = pltpu.SemaphoreType.DMA
    return pl.pallas_call(
        functools.partial(kernel, tiles // colour_matrix.shape[0], tiles),
        out_shape=jax.ShapeDtypeStruct((3, height, slab), F32),
        in_specs=[hbm, hbm, smem, vmem, vmem, vmem, vmem, smem, smem],
        out_specs=vmem,
        scratch_shapes=[
            pltpu.VMEM((CHUNKS, GROUPS, chunk, slab), BF16),
            pltpu.VMEM((2, CHIPS, 3, height, slab), BF16),
            pltpu.VMEM((CHUNKS, CHIPS, 2, chunk, slab), BF16),
            pltpu.VMEM((CHUNKS, CHIPS, 2, chunk, slab), BF16),
            pltpu.VMEM((CHUNKS, CHIPS, 3, chunk, slab), BF16),
            pltpu.VMEM((CHUNKS, CHIPS + 1, 3, chunk, slab), BF16),
            pltpu.VMEM((3, 3 * height, slab), BF16),
            pltpu.VMEM((3, height, slab), BF16),
            pltpu.VMEM((3, height, slab + 2 * HC), BF16),
            dma((CHUNKS, GROUPS)),
            dma((CHUNKS, GROUPS)),
            dma((CHUNKS,)),
            dma((CHIPS,)),
            dma((CHIPS,)),
            dma((CHIPS,)),
            dma((CHUNKS, CHIPS)),
            dma((CHUNKS, CHIPS)),
            dma((CHUNKS, CHIPS)),
            dma((CHUNKS, CHIPS + 1)),
            dma((CHUNKS, 2)),
            dma((CHUNKS, 2)),
            dma((2,)),
            dma((2,)),
        ],
        compiler_params=pltpu.CompilerParams(
            collective_id=0, has_side_effects=True, vmem_limit_bytes=48 * 2**20
        ),
    )(colour, alpha, depth_order, row_taps, row_weights, col_taps, col_weights, colour_matrix, offsets)


def solution(mesh):
    return jax.shard_map(
        shards,
        mesh=mesh,
        in_specs=(
            P("depth", None, "tile", None),
            P("depth", "tile", None),
            P(),
            P(None, "tile"),
            P(None, "tile"),
            P(None, None, "depth"),
            P(None, None, "depth"),
            P(),
            P(),
        ),
        out_specs=P(None, "tile", "depth"),
        check_vma=False,
    )
```

time: 201 us -> 103 us (0.51)
  the two profiles are of different devices: /device:TPU:416 before, /device:TPU:1 now
where the time goes in v1:
time: 103 us
  Pallas kernels  94 us (91%)
  local copies, waits for them, and re-layouts  8.66 us (8%)
    pallas_call x1, Pallas kernels, shards(): pl.pallas_call(functools.partial(kernel, tiles // colour_matrix.shape[0],...  94 us
    unnamed x18, local copies, waits for them, and re-layouts  8.66 us

profile of v1, /device:TPU:1, one launch (start us, length us, event | category | flops | bytes accessed | tf_op | source)
XLA Modules:
  0.0 102.7 jit_solution(12787042020133830665)
XLA Ops:
  0.0 0.7 copy.10.matrix
  0.7 0.0 copy-start
  0.7 1.9 %copy-done = bf16[1,3,128,4096]{3,2,1,0:T(8,128)(2,1)S(1)} copy-done((bf16[1,3,128,4096]{3,2,1,0:T(8,128)(2,1)S(1)}, bf16[1,3,128,4096]{3,2,1,0:T(8,128)(2,1)}, u32[]{:S(2)}) %copy-start) | copy-done | bytes 3145752
  2.6 0.0 copy-start.1
  2.6 1.2 %copy-done.1 = bf16[1,128,4096]{2,1,0:T(8,128)(2,1)S(1)} copy-done((bf16[1,128,4096]{2,1,0:T(8,128)(2,1)S(1)}, bf16[1,128,4096]{2,1,0:T(8,128)(2,1)}, u32[]{:S(2)}) %copy-start.1) | copy-done | bytes 1048600
  3.8 0.0 copy-start.2
  3.8 0.7 copy-done.2
  4.5 0.0 copy-start.3
  4.5 0.7 copy-done.3
  5.2 0.0 copy-start.4
  5.2 0.7 copy-done.4
  5.9 0.0 copy-start.5
  5.9 0.7 copy-done.5
  6.6 0.0 copy-start.6
  6.6 0.7 copy-done.6
  7.3 0.0 copy-start.7
  7.3 0.7 copy-done.7
  7.9 94.0 %shard_map.91 = f32[3,128,256]{2,1,0:T(8,128)S(1)} custom-call(bf16[1,3,128,4096]{3,2,1,0:T(8,128)(2,1)S(1)} %copy-done, bf16[1,128,4096]{2,1,0:T(8,128)(2,1)S(1)} %copy-done.1, s32[16]{0:T(128)S(1)} %copy-done.7, s32[4,128]{1,0:T(4,128)S(1)} %copy-done.4, bf16[4,128]{1,0:T(4,128)(2,1)S(1)} %copy-done.6, s32[4,4,256]{2,1,0:T(4,128)S(1)} %copy-done.2, ...), custom_call_target="tpu_custom_call" | custom-call | tf_op jit(solution)/shard_map/pallas_call | solution.py:367
  101.9 0.7 copy.12
Async XLA Ops:
  0.7 1.9 %copy-start = (bf16[1,3,128,4096]{3,2,1,0:T(8,128)(2,1)S(1)}, bf16[1,3,128,4096]{3,2,1,0:T(8,128)(2,1)}, u32[]{:S(2)}) copy-start(bf16[1,3,128,4096]{3,2,1,0:T(8,128)(2,1)} %colour.1) | copy-start | bytes 9437188
  2.6 1.2 %copy-start.1 = (bf16[1,128,4096]{2,1,0:T(8,128)(2,1)S(1)}, bf16[1,128,4096]{2,1,0:T(8,128)(2,1)}, u32[]{:S(2)}) copy-start(bf16[1,128,4096]{2,1,0:T(8,128)(2,1)} %alpha.1) | copy-start | bytes 3145732
  3.8 0.7 copy-start.2
  4.5 0.7 copy-start.3
  5.2 0.7 copy-start.4
  5.9 0.7 copy-start.5
  6.6 0.7 copy-start.6
  7.3 0.7 copy-start.7

commit v2 on v1

--- a/solution.py
+++ b/solution.py
@@ -32,11 +32,13 @@
 def kernel(
     bands_per_projector,
     tiles,
-    colour, alpha, order, row_taps, row_weights, col_taps, col_weights, matrix, offsets,
+    colour, alpha, order_in, row_taps_in, row_weights_in, col_taps_in, col_weights_in, matrix_in,
+    offsets_in,
     out,
+    order, row_taps, row_weights, col_taps, col_weights, matrix, offsets,
     opac, cols, remain_out, remain_in, part_out, part_in, window, low, vert,
     a_send, a_recv, a_own, c_own, c_send, c_recv, r_send, r_recv, p_send, p_recv,
-    h_send, h_recv, v_send, v_recv,
+    h_send, h_recv, v_send, v_recv, s_own,
 ):
     height, slab = out.shape[1], out.shape[2]
     chunk = height // CHUNKS
@@ -84,6 +86,20 @@
 
         lax.fori_loop(0, n, step, 0)
 
+    small = [
+        pltpu.make_async_copy(source, target, s_own.at[i])
+        for i, (source, target) in enumerate((
+            (order_in, order),
+            (row_taps_in, row_taps),
+            (row_weights_in, row_weights),
+            (col_taps_in, col_taps),
+            (col_weights_in, col_weights),
+            (matrix_in, matrix),
+            (offsets_in, offsets),
+        ))
+    ]
+    for copy in small:
+        copy.start()
     loop(CHUNKS, lambda k: own_alpha(k).start())
     loop(CHIPS, lambda s: own_colour(s).start())
     pl.semaphore_wait(barrier, GROUPS + 1)
@@ -200,6 +216,8 @@
     every(1, GROUPS, lambda k, i: send_alpha(k, i).start())
     loop(CHIPS, lambda s: send_colour(s).start())
 
+    for copy in small:
+        copy.wait()
     flips = [(order[0] // (1 << bit)) % 2 for bit in range(4)]
 
     def in_front(bit, value, hidden):
@@ -337,9 +355,9 @@
         jnp.dot(vert[channel], col_picks, preferred_element_type=F32) * ramp for channel in range(3)
     ]
     for channel in range(3):
-        mixed = matrix[p, channel, 0] * blended[0]
-        mixed += matrix[p, channel, 1] * blended[1]
-        mixed += matrix[p, channel, 2] * blended[2]
+        mixed = matrix[channel, p, 0] * blended[0]
+        mixed += matrix[channel, p, 1] * blended[1]
+        mixed += matrix[channel, p, 2] * blended[2]
         out[channel] = mixed + offsets[p, channel]
 
     every(1, GROUPS, lambda k, i: send_alpha(k, i).wait_send())
@@ -362,14 +380,21 @@
     chunk = height // CHUNKS
     hbm = pl.BlockSpec(memory_space=pltpu.HBM)
     vmem = pl.BlockSpec(memory_space=pltpu.VMEM)
-    smem = pl.BlockSpec(memory_space=pltpu.SMEM)
+    matrix = jnp.transpose(colour_matrix, (1, 0, 2))
     dma = pltpu.SemaphoreType.DMA
     return pl.pallas_call(
         functools.partial(kernel, tiles // colour_matrix.shape[0], tiles),
         out_shape=jax.ShapeDtypeStruct((3, height, slab), F32),
-        in_specs=[hbm, hbm, smem, vmem, vmem, vmem, vmem, smem, smem],
+        in_specs=[hbm] * 9,
         out_specs=vmem,
         scratch_shapes=[
+            pltpu.SMEM(depth_order.shape, depth_order.dtype),
+            pltpu.VMEM(row_taps.shape, row_taps.dtype),
+            pltpu.VMEM(row_weights.shape, row_weights.dtype),
+            pltpu.VMEM(col_taps.shape, col_taps.dtype),
+            pltpu.VMEM(col_weights.shape, col_weights.dtype),
+            pltpu.SMEM(matrix.shape, matrix.dtype),
+            pltpu.SMEM(offsets.shape, offsets.dtype),
             pltpu.VMEM((CHUNKS, GROUPS, chunk, slab), BF16),
             pltpu.VMEM((2, CHIPS, 3, height, slab), BF16),
             pltpu.VMEM((CHUNKS, CHIPS, 2, chunk, slab), BF16),
@@ -393,11 +418,12 @@
             dma((CHUNKS, 2)),
             dma((2,)),
             dma((2,)),
+            dma((7,)),
         ],
         compiler_params=pltpu.CompilerParams(
-            collective_id=0, has_side_effects=True, vmem_limit_bytes=48 * 2**20
+            collective_id=0, has_side_effects=True, vmem_limit_bytes=63 * 2**20
         ),
-    )(colour, alpha, depth_order, row_taps, row_weights, col_taps, col_weights, colour_matrix, offsets)
+    )(colour, alpha, depth_order, row_taps, row_weights, col_taps, col_weights, matrix, offsets)
 
 
 def solution(mesh):

time: 103 us -> 96.2 us (0.934)
  local copies, waits for them, and re-layouts: 8.66 us -> 1.77 us
    unnamed x18 -> x1, local copies, waits for them, and re-layouts: 8.66 us -> 1.77 us
where the time goes in v2:
time: 96.2 us; the launch traced here: 96.1 us
  Pallas kernels  94.3 us (98%)
  local copies, waits for them, and re-layouts  1.77 us (2%)
    pallas_call x1, Pallas kernels, shards(): pl.pallas_call(functools.partial(kernel, tiles // colour_matrix.shape[0],...  94.3 us

profile of v2, /device:TPU:1, one launch (start us, length us, event | category | flops | bytes accessed | tf_op | source)
XLA Modules:
  0.0 96.1 jit_solution(4389746462811275224)
XLA Ops:
  0.0 94.3 %shard_map.91 = f32[3,128,256]{2,1,0:T(8,128)} custom-call(bf16[1,3,128,4096]{3,2,1,0:T(8,128)(2,1)} %colour.1, bf16[1,128,4096]{2,1,0:T(8,128)(2,1)} %alpha.1, s32[16]{0:T(128)} %order_in.1, s32[4,128]{1,0:T(4,128)} %row_taps_in.1, bf16[4,128]{1,0:T(4,128)(2,1)} %row_weights_in.1, s32[4,4,256]{2,1,0:T(4,128)} %col_taps_in.1, ...), custom_call_target="tpu_custom_call" | custom-call | tf_op jit(solution)/shard_map/pallas_call | solution.py:385
  94.3 1.8 %copy.11 = f32[3,128,256]{2,1,0:T(8,128)} copy(f32[3,128,256]{2,1,0:T(8,128)} %shard_map.91) | data formatting | bytes 786432

commit v3 on v2

--- a/solution.py
+++ b/solution.py
@@ -36,7 +36,7 @@
     offsets_in,
     out,
     order, row_taps, row_weights, col_taps, col_weights, matrix, offsets,
-    opac, cols, remain_out, remain_in, part_out, part_in, window, low, vert,
+    opac, cols, left_all, kept, remain_out, remain_in, part_out, part_in, window, low, vert, row_picks, col_matrix,
     a_send, a_recv, a_own, c_own, c_send, c_recv, r_send, r_recv, p_send, p_recv,
     h_send, h_recv, v_send, v_recv, s_own,
 ):
@@ -148,9 +148,10 @@
 
     def send_remain(k, j):
         to = chip(sigma * j)
-        return pltpu.make_async_remote_copy(
-            src_ref=remain_out.at[k, to],
-            dst_ref=remain_in.at[k, j],
+        first = 1 if j in (4, 5) else 0
+        return pltpu.make_async_remote_copy(
+            src_ref=remain_out.at[k, j, pl.ds(first, 2 - first)],
+            dst_ref=remain_in.at[k, j, pl.ds(first, 2 - first)],
             send_sem=r_send.at[k, j],
             recv_sem=r_recv.at[k, j],
             device_id=(2 * to + c, t),
@@ -219,6 +220,24 @@
     for copy in small:
         copy.wait()
     flips = [(order[0] // (1 << bit)) % 2 for bit in range(4)]
+
+    place = lax.broadcasted_iota(jnp.int32, (3 * height, height), 0)
+    picks = jnp.zeros((3 * height, height), F32)
+    for tap in range(4):
+        taps = row_taps[tap, :][None, :]
+        picks += jnp.where(taps == place, row_weights[tap, :].astype(F32)[None, :], 0.0)
+    outside = ((place < height) & (t == 0)) | ((place >= 2 * height) & (t == tiles - 1))
+    row_picks[...] = jnp.transpose(jnp.where(outside, 0.0, picks)).astype(BF16)
+
+    width = slab + 2 * HC
+    p = t // bands_per_projector
+    place = lax.broadcasted_iota(jnp.int32, (width, slab), 0) + (d * slab - HC)
+    col_picks = jnp.zeros((width, slab), F32)
+    for tap in range(4):
+        taps = col_taps[p, tap, :][None, :]
+        col_picks += jnp.where(taps == place, col_weights[p, tap, :].astype(F32)[None, :], 0.0)
+    col_matrix[...] = col_picks.astype(BF16)
+
 
     def in_front(bit, value, hidden):
         return jnp.where(flips[bit] == value, 1.0, hidden)
@@ -245,16 +264,29 @@
             left = [left[g % 2] * in_front(1, g // 2, four[g ^ 2]) for g in range(4)]
             left = [left[g % 4] * in_front(2, g // 4, eight[g ^ 4]) for g in range(8)]
             for g in range(GROUPS):
-                value = left[g % 8] * in_front(3, g // 8, clear[g ^ 8])
-                remain_out[(k, g // 2, g % 2) + place] = (value * value).astype(BF16)
+                left_all[g] = left[g % 8] * in_front(3, g // 8, clear[g ^ 8])
+            kept[(k, 0) + place] = left_all[2 * y]
+            kept[(k, 1) + place] = left_all[2 * y + 1]
+            for j, ends in (((4, 3, 2, 1), 2), ((5, 6, 7), 3)):
+                scale = left_all[2 * chip(sigma * j[0])]
+                kept[(k, ends) + place] = scale
+                scale = 1.0 / scale
+                for i in j:
+                    for core in range(2):
+                        if i != j[0] or core:
+                            value = left_all[2 * chip(sigma * i) + core] * scale
+                            remain_out[(k, i, core) + place] = (value * value).astype(BF16)
 
         loop(blocks, block)
-        loop(CHIPS - 1, lambda i: send_remain(k, i + 1).start())
+        for j in STEPS:
+            send_remain(k, j).start()
 
     loop(CHUNKS, remains)
 
     loop(CHIPS, lambda s: own_colour(s).wait())
     loop(CHIPS, lambda s: recv_colour(s).wait_recv())
+    loop(CHIPS, lambda s: send_colour(s).wait_send())
+    every(1, GROUPS, lambda k, i: send_alpha(k, i).wait_send())
 
     def add_step(j):
         s = chip(-sigma * j)
@@ -268,10 +300,13 @@
                 row, lane = block_at(b)
                 place = (pl.ds(row, TILE_ROWS), pl.ds(lane, LANES))
                 whole = (pl.ds(pl.multiple_of(k * chunk + row, TILE_ROWS), TILE_ROWS), pl.ds(lane, LANES))
-                first = root(remain_in[(k, j, 0) + place])
+                if j not in (4, 5):
+                    first = root(remain_in[(k, j, 0) + place])
                 second = root(remain_in[(k, j, 1) + place])
                 for channel in range(3):
-                    total = first * cols[(0, s, channel) + whole].astype(F32)
+                    total = cols[(0, s, channel) + whole].astype(F32)
+                    if j not in (4, 5):
+                        total = first * total
                     total += second * cols[(1, s, channel) + whole].astype(F32)
                     if j not in (4, 5):
                         total += root(part_in[(k, j, channel) + place])
@@ -295,13 +330,13 @@
             whole_row = pl.multiple_of(k * chunk + row, TILE_ROWS)
             whole = (pl.ds(whole_row, TILE_ROWS), pl.ds(lane, LANES))
             middle = (pl.ds(pl.multiple_of(height + whole_row, TILE_ROWS), TILE_ROWS), pl.ds(lane, LANES))
-            first = root(remain_out[(k, y, 0) + place])
-            second = root(remain_out[(k, y, 1) + place])
+            first, second = kept[(k, 0) + place], kept[(k, 1) + place]
+            far, near = kept[(k, 2) + place], kept[(k, 3) + place]
             for channel in range(3):
                 total = first * cols[(0, y, channel) + whole].astype(F32)
                 total += second * cols[(1, y, channel) + whole].astype(F32)
-                total += root(part_in[(k, 0, channel) + place])
-                total += root(part_in[(k, 8, channel) + place])
+                total += far * root(part_in[(k, 0, channel) + place])
+                total += near * root(part_in[(k, 8, channel) + place])
                 high = total.astype(BF16)
                 window[(channel,) + middle] = high
                 low[(channel,) + whole] = (total - high.astype(F32)).astype(BF16)
@@ -312,22 +347,9 @@
 
     loop(CHUNKS, finish)
 
-    place = lax.broadcasted_iota(jnp.int32, (3 * height, height), 0)
-    picks = jnp.zeros((3 * height, height), F32)
-    for tap in range(4):
-        taps = row_taps[tap, :][None, :]
-        picks += jnp.where(taps == place, row_weights[tap, :].astype(F32)[None, :], 0.0)
-    outside = ((place < height) & (t == 0)) | ((place >= 2 * height) & (t == tiles - 1))
-    picks = jnp.transpose(jnp.where(outside, 0.0, picks)).astype(BF16)
-
-    width = slab + 2 * HC
-    p = t // bands_per_projector
-    place = lax.broadcasted_iota(jnp.int32, (width, slab), 0) + (d * slab - HC)
-    col_picks = jnp.zeros((width, slab), F32)
-    for tap in range(4):
-        taps = col_taps[p, tap, :][None, :]
-        col_picks += jnp.where(taps == place, col_weights[p, tap, :].astype(F32)[None, :], 0.0)
-    col_picks = col_picks.astype(BF16)
+    for j in STEPS:
+        loop(CHUNKS, lambda k: send_remain(k, j).wait_send())
+        loop(CHUNKS, lambda k: send_part(k, j).wait_send())
 
     def wait_halo(k):
         send_halo(k, 0).wait_recv()
@@ -336,8 +358,8 @@
     loop(CHUNKS, wait_halo)
 
     for channel in range(3):
-        value = jnp.dot(picks, window[channel], preferred_element_type=F32)
-        value += jnp.dot(picks[:, height : 2 * height], low[channel], preferred_element_type=F32)
+        value = jnp.dot(row_picks[...], window[channel], preferred_element_type=F32)
+        value += jnp.dot(row_picks[:, height : 2 * height], low[channel], preferred_element_type=F32)
         vert[channel, :, HC : HC + slab] = value.astype(BF16)
     send_beside(0).start()
     send_beside(1).start()
@@ -352,7 +374,7 @@
     send_beside(0).wait_recv()
     send_beside(1).wait_recv()
     blended = [
-        jnp.dot(vert[channel], col_picks, preferred_element_type=F32) * ramp for channel in range(3)
+        jnp.dot(vert[channel], col_matrix[...], preferred_element_type=F32) * ramp for channel in range(3)
     ]
     for channel in range(3):
         mixed = matrix[channel, p, 0] * blended[0]
@@ -360,11 +382,6 @@
         mixed += matrix[channel, p, 2] * blended[2]
         out[channel] = mixed + offsets[p, channel]
 
-    every(1, GROUPS, lambda k, i: send_alpha(k, i).wait_send())
-    loop(CHIPS, lambda s: send_colour(s).wait_send())
-    every(1, CHIPS, lambda k, j: send_remain(k, j).wait_send())
-    for j in STEPS:
-        loop(CHUNKS, lambda k: send_part(k, j).wait_send())
     loop(CHUNKS, lambda k: send_halo(k, 0).wait_send())
     loop(CHUNKS, lambda k: send_halo(k, 1).wait_send())
     send_beside(0).wait_send()
@@ -397,6 +414,8 @@
             pltpu.SMEM(offsets.shape, offsets.dtype),
             pltpu.VMEM((CHUNKS, GROUPS, chunk, slab), BF16),
             pltpu.VMEM((2, CHIPS, 3, height, slab), BF16),
+            pltpu.VMEM((GROUPS, TILE_ROWS, LANES), F32),
+            pltpu.VMEM((CHUNKS, 4, chunk, slab), F32),
             pltpu.VMEM((CHUNKS, CHIPS, 2, chunk, slab), BF16),
             pltpu.VMEM((CHUNKS, CHIPS, 2, chunk, slab), BF16),
             pltpu.VMEM((CHUNKS, CHIPS, 3, chunk, slab), BF16),
@@ -404,6 +423,8 @@
             pltpu.VMEM((3, 3 * height, slab), BF16),
             pltpu.VMEM((3, height, slab), BF16),
             pltpu.VMEM((3, height, slab + 2 * HC), BF16),
+            pltpu.VMEM((height, 3 * height), BF16),
+            pltpu.VMEM((slab + 2 * HC, slab), BF16),
             dma((CHUNKS, GROUPS)),
             dma((CHUNKS, GROUPS)),
             dma((CHUNKS,)),

time: 96.2 us -> 88.8 us (0.923)
  Pallas kernels: 94.3 us -> 86.9 us
    pallas_call x1, Pallas kernels: 94.3 us -> 86.9 us  [shards(): pl.pallas_call(functools.partial(kernel, tiles // colour_matrix.shape[0],...]
where the time goes in v3:
time: 88.8 us; the launch traced here: 88.6 us
  Pallas kernels  86.9 us (98%)
  local copies, waits for them, and re-layouts  1.77 us (2%)
    pallas_call x1, Pallas kernels, shards(): pl.pallas_call(functools.partial(kernel, tiles // colour_matrix.shape[0],...  86.9 us

profile of v3, /device:TPU:1, one launch (start us, length us, event | category | flops | bytes accessed | tf_op | source)
XLA Modules:
  0.0 88.6 jit_solution(15455826462105349837)
XLA Ops:
  0.0 86.9 %shard_map.91 = f32[3,128,256]{2,1,0:T(8,128)} custom-call(bf16[1,3,128,4096]{3,2,1,0:T(8,128)(2,1)} %colour.1, bf16[1,128,4096]{2,1,0:T(8,128)(2,1)} %alpha.1, s32[16]{0:T(128)} %order_in.1, s32[4,128]{1,0:T(4,128)} %row_taps_in.1, bf16[4,128]{1,0:T(4,128)(2,1)} %row_weights_in.1, s32[4,4,256]{2,1,0:T(4,128)} %col_taps_in.1, ...), custom_call_target="tpu_custom_call" | custom-call | tf_op jit(solution)/shard_map/pallas_call | solution.py:402
  86.9 1.8 %copy.11 = f32[3,128,256]{2,1,0:T(8,128)} copy(f32[3,128,256]{2,1,0:T(8,128)} %shard_map.91) | data formatting | bytes 786432

commit v4 on v3

--- a/solution.py
+++ b/solution.py
@@ -36,7 +36,8 @@
     offsets_in,
     out,
     order, row_taps, row_weights, col_taps, col_weights, matrix, offsets,
-    opac, cols, left_all, kept, remain_out, remain_in, part_out, part_in, window, low, vert, row_picks, col_matrix,
+    opac, cols, left_all, kept, remain_out, remain_in, part_out, part_in, window, low, vert,
+    row_picks, col_matrix, partial,
     a_send, a_recv, a_own, c_own, c_send, c_recv, r_send, r_recv, p_send, p_recv,
     h_send, h_recv, v_send, v_recv, s_own,
 ):
@@ -191,15 +192,15 @@
             device_id_type=MESH,
         )
 
-    def send_beside(side):
+    def send_beside(channel, side):
         to = (d + GROUPS - 1) % GROUPS if side == 0 else (d + 1) % GROUPS
         source = HC if side == 0 else slab
         target = HC + slab if side == 0 else 0
         return pltpu.make_async_remote_copy(
-            src_ref=vert.at[:, :, pl.ds(source, HC)],
-            dst_ref=vert.at[:, :, pl.ds(target, HC)],
-            send_sem=v_send.at[side],
-            recv_sem=v_recv.at[side],
+            src_ref=vert.at[channel, :, pl.ds(source, HC)],
+            dst_ref=vert.at[channel, :, pl.ds(target, HC)],
+            send_sem=v_send.at[channel, side],
+            recv_sem=v_recv.at[channel, side],
             device_id=(to, t),
             device_id_type=MESH,
         )
@@ -355,14 +356,27 @@
         send_halo(k, 0).wait_recv()
         send_halo(k, 1).wait_recv()
 
+    def product(a, b):
+        return jnp.dot(a, b, preferred_element_type=F32)
+
+    for channel in range(3):
+        band = row_picks[:, height : 2 * height]
+        partial[channel] = product(band, window[channel, height : 2 * height]) + product(
+            band, low[channel]
+        )
     loop(CHUNKS, wait_halo)
 
     for channel in range(3):
-        value = jnp.dot(row_picks[...], window[channel], preferred_element_type=F32)
-        value += jnp.dot(row_picks[:, height : 2 * height], low[channel], preferred_element_type=F32)
+        value = partial[channel]
+        value += product(row_picks[:, :height], window[channel, :height])
+        value += product(row_picks[:, 2 * height :], window[channel, 2 * height :])
         vert[channel, :, HC : HC + slab] = value.astype(BF16)
-    send_beside(0).start()
-    send_beside(1).start()
+        for side in range(2):
+            send_beside(channel, side).start()
+    for channel in range(3):
+        partial[channel] = product(
+            vert[channel, :, HC : HC + slab], col_matrix[HC : HC + slab]
+        )
 
     within = (t % bands_per_projector) * height + lax.broadcasted_iota(jnp.int32, (height, slab), 0)
     within = within.astype(F32)
@@ -371,11 +385,14 @@
         1.0, jnp.minimum((within + 0.5) / BLEND, (proj_height - within - 0.5) / BLEND)
     )
 
-    send_beside(0).wait_recv()
-    send_beside(1).wait_recv()
-    blended = [
-        jnp.dot(vert[channel], col_matrix[...], preferred_element_type=F32) * ramp for channel in range(3)
-    ]
+    blended = []
+    for channel in range(3):
+        for side in range(2):
+            send_beside(channel, side).wait_recv()
+        value = partial[channel]
+        value += product(vert[channel, :, :HC], col_matrix[:HC])
+        value += product(vert[channel, :, HC + slab :], col_matrix[HC + slab :])
+        blended.append(value * ramp)
     for channel in range(3):
         mixed = matrix[channel, p, 0] * blended[0]
         mixed += matrix[channel, p, 1] * blended[1]
@@ -384,8 +401,9 @@
 
     loop(CHUNKS, lambda k: send_halo(k, 0).wait_send())
     loop(CHUNKS, lambda k: send_halo(k, 1).wait_send())
-    send_beside(0).wait_send()
-    send_beside(1).wait_send()
+    for channel in range(3):
+        for side in range(2):
+            send_beside(channel, side).wait_send()
 
 
 def shards(
@@ -425,6 +443,7 @@
             pltpu.VMEM((3, height, slab + 2 * HC), BF16),
             pltpu.VMEM((height, 3 * height), BF16),
             pltpu.VMEM((slab + 2 * HC, slab), BF16),
+            pltpu.VMEM((3, height, slab), F32),
             dma((CHUNKS, GROUPS)),
             dma((CHUNKS, GROUPS)),
             dma((CHUNKS,)),
@@ -437,14 +456,19 @@
             dma((CHUNKS, CHIPS + 1)),
             dma((CHUNKS, 2)),
             dma((CHUNKS, 2)),
-            dma((2,)),
-            dma((2,)),
+            dma((3, 2)),
+            dma((3, 2)),
             dma((7,)),
         ],
         compiler_params=pltpu.CompilerParams(
-            collective_id=0, has_side_effects=True, vmem_limit_bytes=63 * 2**20
+            collective_id=0, has_side_effects=True, vmem_limit_bytes=40 * 2**20
         ),
-    )(colour, alpha, depth_order, row_taps, row_weights, col_taps, col_weights, matrix, offsets)
+    )(*[
+        pltpu.with_memory_space_constraint(x, pltpu.HBM)
+        for x in (
+            colour, alpha, depth_order, row_taps, row_weights, col_taps, col_weights, matrix, offsets
+        )
+    ])
 
 
 def solution(mesh):

time: 88.8 us -> 86.8 us (0.977)
  local copies, waits for them, and re-layouts: 1.77 us -> 0.75 us
  Pallas kernels: 86.9 us -> 85.9 us
    unnamed x1, local copies, waits for them, and re-layouts: 1.77 us -> 0.75 us
    pallas_call x1, Pallas kernels: 86.9 us -> 85.9 us  [shards(): pl.pallas_call(functools.partial(kernel, tiles // colour_matrix.shape[0],...]
where the time goes in v4:
time: 86.8 us; the launch traced here: 86.7 us
  Pallas kernels  85.9 us (99%)
    pallas_call x1, Pallas kernels, shards(): pl.pallas_call(functools.partial(kernel, tiles // colour_matrix.shape[0],...  85.9 us

profile of v4, /device:TPU:1, one launch (start us, length us, event | category | flops | bytes accessed | tf_op | source)
XLA Modules:
  0.0 86.7 jit_solution(1434586741608893666)
XLA Ops:
  0.0 85.9 %shard_map.91 = f32[3,128,256]{2,1,0:T(8,128)S(1)} custom-call(bf16[1,3,128,4096]{3,2,1,0:T(8,128)(2,1)} %colour.1, bf16[1,128,4096]{2,1,0:T(8,128)(2,1)} %alpha.1, s32[16]{0:T(128)} %order_in.1, s32[4,128]{1,0:T(4,128)} %row_taps_in.1, bf16[4,128]{1,0:T(4,128)(2,1)} %row_weights_in.1, s32[4,4,256]{2,1,0:T(4,128)} %col_taps_in.1, ...), custom_call_target="tpu_custom_call" | custom-call | tf_op jit(solution)/shard_map/pallas_call | solution.py:420
  85.9 0.7 copy.11

commit v5 on v4

--- a/solution.py
+++ b/solution.py
@@ -12,6 +12,7 @@
 GROUPS = 16
 CHIPS = 8
 CHUNKS = 4
+COARSE = 2
 TILE_ROWS = 16
 LANES = 128
 STEPS = (4, 5, 3, 6, 2, 7, 1)
@@ -43,6 +44,7 @@
 ):
     height, slab = out.shape[1], out.shape[2]
     chunk = height // CHUNKS
+    coarse = height // COARSE
     blocks = (chunk // TILE_ROWS) * (slab // LANES)
     d = lax.axis_index("depth")
     t = lax.axis_index("tile")
@@ -58,7 +60,7 @@
         return pl.ds(pl.multiple_of(device * slab, slab), slab)
 
     def rows_of(k):
-        return pl.ds(pl.multiple_of(k * chunk, chunk), chunk)
+        return pl.ds(pl.multiple_of(k * coarse, coarse), coarse)
 
     barrier = pltpu.get_barrier_semaphore()
 
@@ -101,7 +103,7 @@
     ]
     for copy in small:
         copy.start()
-    loop(CHUNKS, lambda k: own_alpha(k).start())
+    loop(COARSE, lambda k: own_alpha(k).start())
     loop(CHIPS, lambda s: own_colour(s).start())
     pl.semaphore_wait(barrier, GROUPS + 1)
 
@@ -213,7 +215,7 @@
 
             return lax.fori_loop(first, last, inner, 0)
 
-        lax.fori_loop(0, CHUNKS, outer, 0)
+        lax.fori_loop(0, COARSE, outer, 0)
 
     every(1, GROUPS, lambda k, i: send_alpha(k, i).start())
     loop(CHIPS, lambda s: send_colour(s).start())
@@ -278,22 +280,25 @@
                             value = left_all[2 * chip(sigma * i) + core] * scale
                             remain_out[(k, i, core) + place] = (value * value).astype(BF16)
 
-        loop(blocks, block)
+        loop(blocks * (CHUNKS // COARSE), block)
         for j in STEPS:
             send_remain(k, j).start()
 
-    loop(CHUNKS, remains)
+    loop(COARSE, remains)
 
     loop(CHIPS, lambda s: own_colour(s).wait())
     loop(CHIPS, lambda s: recv_colour(s).wait_recv())
     loop(CHIPS, lambda s: send_colour(s).wait_send())
     every(1, GROUPS, lambda k, i: send_alpha(k, i).wait_send())
 
+    def within_coarse(k, row, lane):
+        start = (k % (CHUNKS // COARSE)) * chunk + row
+        return (pl.ds(pl.multiple_of(start, TILE_ROWS), TILE_ROWS), pl.ds(lane, LANES))
+
     def add_step(j):
         s = chip(-sigma * j)
 
-        def of_chunk(k):
-            send_remain(k, j).wait_recv()
+        def of_chunk(q, k):
             if j not in (4, 5):
                 recv_part(k, j).wait_recv()
 
@@ -301,9 +306,10 @@
                 row, lane = block_at(b)
                 place = (pl.ds(row, TILE_ROWS), pl.ds(lane, LANES))
                 whole = (pl.ds(pl.multiple_of(k * chunk + row, TILE_ROWS), TILE_ROWS), pl.ds(lane, LANES))
+                inner = within_coarse(k, row, lane)
                 if j not in (4, 5):
-                    first = root(remain_in[(k, j, 0) + place])
-                second = root(remain_in[(k, j, 1) + place])
+                    first = root(remain_in[(q, j, 0) + inner])
+                second = root(remain_in[(q, j, 1) + inner])
                 for channel in range(3):
                     total = cols[(0, s, channel) + whole].astype(F32)
                     if j not in (4, 5):
@@ -316,10 +322,16 @@
             loop(blocks, block)
             send_part(k, j).start()
 
-        loop(CHUNKS, of_chunk)
-
-    for j in STEPS:
-        add_step(j)
+        def at(k):
+            if k % (CHUNKS // COARSE) == 0:
+                send_remain(k // (CHUNKS // COARSE), j).wait_recv()
+            of_chunk(k // (CHUNKS // COARSE), k)
+
+        return at
+
+    bodies = [add_step(j) for j in STEPS]
+    for _, k, i in sorted((i + 0.5 * k, k, i) for i in range(7) for k in range(CHUNKS)):
+        bodies[i](k)
 
     def finish(k):
         recv_part(k, 0).wait_recv()
@@ -331,8 +343,10 @@
             whole_row = pl.multiple_of(k * chunk + row, TILE_ROWS)
             whole = (pl.ds(whole_row, TILE_ROWS), pl.ds(lane, LANES))
             middle = (pl.ds(pl.multiple_of(height + whole_row, TILE_ROWS), TILE_ROWS), pl.ds(lane, LANES))
-            first, second = kept[(k, 0) + place], kept[(k, 1) + place]
-            far, near = kept[(k, 2) + place], kept[(k, 3) + place]
+            q = k // (CHUNKS // COARSE)
+            inner = within_coarse(k, row, lane)
+            first, second = kept[(q, 0) + inner], kept[(q, 1) + inner]
+            far, near = kept[(q, 2) + inner], kept[(q, 3) + inner]
             for channel in range(3):
                 total = first * cols[(0, y, channel) + whole].astype(F32)
                 total += second * cols[(1, y, channel) + whole].astype(F32)
@@ -349,7 +363,7 @@
     loop(CHUNKS, finish)
 
     for j in STEPS:
-        loop(CHUNKS, lambda k: send_remain(k, j).wait_send())
+        loop(COARSE, lambda k: send_remain(k, j).wait_send())
         loop(CHUNKS, lambda k: send_part(k, j).wait_send())
 
     def wait_halo(k):
@@ -389,10 +403,14 @@
     for channel in range(3):
         for side in range(2):
             send_beside(channel, side).wait_recv()
-        value = partial[channel]
-        value += product(vert[channel, :, :HC], col_matrix[:HC])
-        value += product(vert[channel, :, HC + slab :], col_matrix[HC + slab :])
-        blended.append(value * ramp)
+        value = jnp.concatenate(
+            [
+                product(vert[channel, :, :HC], col_matrix[:HC, :HC]),
+                product(vert[channel, :, HC + slab :], col_matrix[HC + slab :, HC:]),
+            ],
+            axis=1,
+        )
+        blended.append((partial[channel] + value) * ramp)
     for channel in range(3):
         mixed = matrix[channel, p, 0] * blended[0]
         mixed += matrix[channel, p, 1] * blended[1]
@@ -412,7 +430,7 @@
     tiles = lax.axis_size("tile")
     height = colour.shape[2]
     slab = colour.shape[3] // GROUPS
-    chunk = height // CHUNKS
+    chunk, coarse = height // CHUNKS, height // COARSE
     hbm = pl.BlockSpec(memory_space=pltpu.HBM)
     vmem = pl.BlockSpec(memory_space=pltpu.VMEM)
     matrix = jnp.transpose(colour_matrix, (1, 0, 2))
@@ -430,12 +448,12 @@
             pltpu.VMEM(col_weights.shape, col_weights.dtype),
             pltpu.SMEM(matrix.shape, matrix.dtype),
             pltpu.SMEM(offsets.shape, offsets.dtype),
-            pltpu.VMEM((CHUNKS, GROUPS, chunk, slab), BF16),
+            pltpu.VMEM((COARSE, GROUPS, coarse, slab), BF16),
             pltpu.VMEM((2, CHIPS, 3, height, slab), BF16),
             pltpu.VMEM((GROUPS, TILE_ROWS, LANES), F32),
-            pltpu.VMEM((CHUNKS, 4, chunk, slab), F32),
-            pltpu.VMEM((CHUNKS, CHIPS, 2, chunk, slab), BF16),
-            pltpu.VMEM((CHUNKS, CHIPS, 2, chunk, slab), BF16),
+            pltpu.VMEM((COARSE, 4, coarse, slab), F32),
+            pltpu.VMEM((COARSE, CHIPS, 2, coarse, slab), BF16),
+            pltpu.VMEM((COARSE, CHIPS, 2, coarse, slab), BF16),
             pltpu.VMEM((CHUNKS, CHIPS, 3, chunk, slab), BF16),
             pltpu.VMEM((CHUNKS, CHIPS + 1, 3, chunk, slab), BF16),
             pltpu.VMEM((3, 3 * height, slab), BF16),
@@ -444,14 +462,14 @@
             pltpu.VMEM((height, 3 * height), BF16),
             pltpu.VMEM((slab + 2 * HC, slab), BF16),
             pltpu.VMEM((3, height, slab), F32),
-            dma((CHUNKS, GROUPS)),
-            dma((CHUNKS, GROUPS)),
-            dma((CHUNKS,)),
+            dma((COARSE, GROUPS)),
+            dma((COARSE, GROUPS)),
+            dma((COARSE,)),
             dma((CHIPS,)),
             dma((CHIPS,)),
             dma((CHIPS,)),
-            dma((CHUNKS, CHIPS)),
-            dma((CHUNKS, CHIPS)),
+            dma((COARSE, CHIPS)),
+            dma((COARSE, CHIPS)),
             dma((CHUNKS, CHIPS)),
             dma((CHUNKS, CHIPS + 1)),
             dma((CHUNKS, 2)),

time: 86.8 us -> 85.8 us (0.988)
  Pallas kernels: 85.9 us -> 84.9 us
    pallas_call x1, Pallas kernels: 85.9 us -> 84.9 us  [shards(): pl.pallas_call(functools.partial(kernel, tiles // colour_matrix.shape[0],...]
where the time goes in v5:
time: 85.8 us; the launch traced here: 85.7 us
  Pallas kernels  84.9 us (99%)
    pallas_call x1, Pallas kernels, shards(): pl.pallas_call(functools.partial(kernel, tiles // colour_matrix.shape[0],...  84.9 us

profile of v5, /device:TPU:1, one launch (start us, length us, event | category | flops | bytes accessed | tf_op | source)
XLA Modules:
  0.0 85.7 jit_solution(5186887041238564123)
XLA Ops:
  0.0 84.9 %shard_map.91 = f32[3,128,256]{2,1,0:T(8,128)S(1)} custom-call(bf16[1,3,128,4096]{3,2,1,0:T(8,128)(2,1)} %colour.1, bf16[1,128,4096]{2,1,0:T(8,128)(2,1)} %alpha.1, s32[16]{0:T(128)} %order_in.1, s32[4,128]{1,0:T(4,128)} %row_taps_in.1, bf16[4,128]{1,0:T(4,128)(2,1)} %row_weights_in.1, s32[4,4,256]{2,1,0:T(4,128)} %col_taps_in.1, ...), custom_call_target="tpu_custom_call" | custom-call | tf_op jit(solution)/shard_map/pallas_call | solution.py:438
  84.9 0.7 copy.11

commit v6 on v5

--- a/solution.py
+++ b/solution.py
@@ -101,10 +101,6 @@
             (offsets_in, offsets),
         ))
     ]
-    for copy in small:
-        copy.start()
-    loop(COARSE, lambda k: own_alpha(k).start())
-    loop(CHIPS, lambda s: own_colour(s).start())
     pl.semaphore_wait(barrier, GROUPS + 1)
 
     def send_alpha(k, i):
@@ -218,6 +214,10 @@
         lax.fori_loop(0, COARSE, outer, 0)
 
     every(1, GROUPS, lambda k, i: send_alpha(k, i).start())
+    for copy in small:
+        copy.start()
+    loop(COARSE, lambda k: own_alpha(k).start())
+    loop(CHIPS, lambda s: own_colour(s).start())
     loop(CHIPS, lambda s: send_colour(s).start())
 
     for copy in small:
@@ -329,10 +329,6 @@
 
         return at
 
-    bodies = [add_step(j) for j in STEPS]
-    for _, k, i in sorted((i + 0.5 * k, k, i) for i in range(7) for k in range(CHUNKS)):
-        bodies[i](k)
-
     def finish(k):
         recv_part(k, 0).wait_recv()
         recv_part(k, 8).wait_recv()
@@ -360,7 +356,10 @@
         send_halo(k, 0).start()
         send_halo(k, 1).start()
 
-    loop(CHUNKS, finish)
+    bodies = [add_step(j) for j in STEPS] + [finish]
+    places = list(range(7)) + [7.8]
+    for _, k, i in sorted((places[i] + 0.7 * k, k, i) for i in range(8) for k in range(CHUNKS)):
+        bodies[i](k)
 
     for j in STEPS:
         loop(COARSE, lambda k: send_remain(k, j).wait_send())

time: 85.8 us -> 85.5 us (level)
  no operation moved by 1% of the time
where the time goes in v6:
time: 85.5 us; the launch traced here: 85.4 us
  Pallas kernels  84.7 us (99%)
    pallas_call x1, Pallas kernels, shards(): pl.pallas_call(functools.partial(kernel, tiles // colour_matrix.shape[0],...  84.7 us

profile of v6, /device:TPU:1, one launch (start us, length us, event | category | flops | bytes accessed | tf_op | source)
XLA Modules:
  0.0 85.4 jit_solution(9657585838019487417)
XLA Ops:
  0.0 84.7 %shard_map.91 = f32[3,128,256]{2,1,0:T(8,128)S(1)} custom-call(bf16[1,3,128,4096]{3,2,1,0:T(8,128)(2,1)} %colour.1, bf16[1,128,4096]{2,1,0:T(8,128)(2,1)} %alpha.1, s32[16]{0:T(128)} %order_in.1, s32[4,128]{1,0:T(4,128)} %row_taps_in.1, bf16[4,128]{1,0:T(4,128)(2,1)} %row_weights_in.1, s32[4,4,256]{2,1,0:T(4,128)} %col_taps_in.1, ...), custom_call_target="tpu_custom_call" | custom-call | tf_op jit(solution)/shard_map/pallas_call | solution.py:437
  84.7 0.7 copy.11

commit v7 on v5

--- a/solution.py
+++ b/solution.py
@@ -330,7 +330,7 @@
         return at
 
     bodies = [add_step(j) for j in STEPS]
-    for _, k, i in sorted((i + 0.5 * k, k, i) for i in range(7) for k in range(CHUNKS)):
+    for _, k, i in sorted((i + 0.7 * k, k, i) for i in range(7) for k in range(CHUNKS)):
         bodies[i](k)
 
     def finish(k):

time: 85.8 us -> 85.5 us (level)
  no operation moved by 1% of the time
where the time goes in v7:
time: 85.5 us; the launch traced here: 85.4 us
  Pallas kernels  84.7 us (99%)
    pallas_call x1, Pallas kernels, shards(): pl.pallas_call(functools.partial(kernel, tiles // colour_matrix.shape[0],...  84.7 us

profile of v7, /device:TPU:1, one launch (start us, length us, event | category | flops | bytes accessed | tf_op | source)
XLA Modules:
  0.0 85.4 jit_solution(17240560372957934338)
XLA Ops:
  0.0 84.7 %shard_map.91 = f32[3,128,256]{2,1,0:T(8,128)S(1)} custom-call(bf16[1,3,128,4096]{3,2,1,0:T(8,128)(2,1)} %colour.1, bf16[1,128,4096]{2,1,0:T(8,128)(2,1)} %alpha.1, s32[16]{0:T(128)} %order_in.1, s32[4,128]{1,0:T(4,128)} %row_taps_in.1, bf16[4,128]{1,0:T(4,128)(2,1)} %row_weights_in.1, s32[4,4,256]{2,1,0:T(4,128)} %col_taps_in.1, ...), custom_call_target="tpu_custom_call" | custom-call | tf_op jit(solution)/shard_map/pallas_call | solution.py:438
  84.7 0.7 copy.11
